TPU v7x, 128 devices: a whole 4x4x4 slice. The times are simulated.
128 devices in a mesh: seq: 32 (over y, x, core), heads: 4 (over z).
Axes of the slice: x: 4, y: 4, z: 4, core: 2. Of those that a mesh axis runs over, the one named last changes fastest.
Arguments:
- queries: bfloat16 [8192, 4096], P('seq', 'heads')
- keys: bfloat16 [8192, 4096], P('seq', 'heads')
- values: bfloat16 [8192, 4096], P('seq', 'heads'), may hold values from -6 to 6
- cca_queries: bfloat16 [8192, 4096], P('seq', 'heads')
- token_table: bfloat16 [128000, 2, 4096], P(('seq', 'heads'))
- neighbour_ids: int32 [128, 2, 128], P(('seq', 'heads')), may hold values from 0 to 127999, as said below
- doc_lengths: int32 [32], replicated, may hold values from 1 to 1792, 8192 in all
Outputs:
- attention_out: bfloat16 [8192, 4096], P('seq', 'heads')
- cca_out: bfloat16 [8192, 4096], P('seq', 'heads')
Inputs may be any that keep to these rules, and one draw needn't show every extreme that they name: `neighbour_ids`: the 256 ids held by one device fall at most 4 times into the 1000 table rows of any one device; the rows of one device, the same for all, receive exactly 4 ids from every device. `doc_lengths`: the longest document has exactly 1792 tokens.
All inputs are finite; a program needn't handle non-finite values.
Results may differ from a plain program's by a relative error of at most 0.0044.
Values may be sent and summed in bfloat16 or wider, within the bound.
A program may use at most 192 MiB of HBM per device.

v0:
```python
import math

import jax
import jax.numpy as jnp
from jax import lax
from jax.sharding import PartitionSpec as P

HS = 128
STRETCH = 64
NEIGH = 2
NLEN = 128


NEG = -1e30


def from_behind(block, axis, distance):
    devices = range(lax.axis_size(axis))
    route = [(i - distance, i) for i in devices if i - distance in devices]
    return lax.ppermute(block, axis, route)


def attend(query, key_block, value_block, allowed):
    scores = jnp.einsum(
        "bqhd,bkhd->bhqk", query, key_block, preferred_element_type=jnp.float32
    ) / math.sqrt(HS)
    scores = jnp.where(allowed[:, None], scores, NEG)
    top = jnp.max(scores, axis=-1, keepdims=True)
    weights = jnp.where(allowed[:, None], jnp.exp(scores - top), 0.0)
    total = jnp.sum(weights, axis=-1)
    mixed = jnp.einsum(
        "bhqk,bkhd->bqhd",
        weights.astype(jnp.bfloat16),
        value_block,
        preferred_element_type=jnp.float32,
    )
    return mixed / jnp.transpose(total, (0, 2, 1))[..., None]


def doc_of(positions, ends):
    return jnp.sum((positions[:, None] >= ends[None, :]).astype(jnp.int32), axis=1)


def slot_plan(flat_ids, owners, slot_cap, shard_rows):
    id_count = flat_ids.shape[0]
    owner = flat_ids // shard_rows
    row_inside = flat_ids - owner * shard_rows
    order = jnp.arange(id_count, dtype=jnp.int32)
    before = (owner[:, None] == owner[None, :]) & (order[None, :] < order[:, None])
    rank = jnp.sum(before.astype(jnp.int32), axis=1)
    slot = owner * slot_cap + rank
    asked = jnp.zeros((owners * slot_cap,), jnp.int32).at[slot].set(row_inside)
    return (slot, asked)


def encode_rows(embedded, id_count, feature_width):
    head_total = feature_width // HS
    groups = id_count // NLEN
    table_keys = embedded[:, 0].reshape(groups, NLEN, head_total, HS)
    table_values = embedded[:, 1].reshape(groups, NLEN, head_total, HS)
    mixed = attend(table_keys, table_keys, table_values, jnp.ones((1, NLEN, NLEN), bool))
    encoded_values = (table_values.astype(jnp.float32) + mixed).astype(jnp.bfloat16)
    encoded = jnp.stack(
        [
            table_keys.reshape(id_count, feature_width),
            encoded_values.reshape(id_count, feature_width),
        ],
        axis=1,
    )
    return encoded.reshape(id_count // (NEIGH * NLEN), NEIGH * NLEN, 2, feature_width)


def body(queries, keys, values, cca_queries, token_table, neighbour_ids, doc_lengths):
    tok_rows = queries.shape[0]
    width = queries.shape[1]
    local_heads = width // HS
    seq_count = lax.axis_size("seq")
    head_count = lax.axis_size("heads")
    look = min(7, seq_count // 2 - 1)
    seq_index = lax.axis_index("seq")
    ends = jnp.cumsum(doc_lengths)
    paired = jnp.stack([keys, values])
    pieces = [paired]
    moving = paired
    for step in range(look):
        moving = from_behind(moving, "seq", 1)
        pieces.insert(0, moving)
    window = jnp.concatenate(pieces, axis=1)
    span_rows = window.shape[1]
    query_pos = seq_index * tok_rows + jnp.arange(tok_rows, dtype=jnp.int32)
    key_pos = (seq_index - look) * tok_rows + jnp.arange(span_rows, dtype=jnp.int32)
    allowed = (key_pos[None, :] <= query_pos[:, None]) & (key_pos[None, :] >= 0)
    allowed = allowed & (doc_of(query_pos, ends)[:, None] == doc_of(key_pos, ends)[None, :])
    query_heads = queries.reshape(1, tok_rows, local_heads, HS)
    key_heads = window[0].reshape(1, span_rows, local_heads, HS)
    value_heads = window[1].reshape(1, span_rows, local_heads, HS)
    results = []
    for first in range(0, local_heads, 2):
        results.append(
            attend(
                query_heads[:, :, first : first + 2],
                key_heads[:, :, first : first + 2],
                value_heads[:, :, first : first + 2],
                allowed[None],
            )
        )
    attention_out = jnp.concatenate(results, axis=2).reshape(tok_rows, width).astype(jnp.bfloat16)
    owners = seq_count * head_count
    shard_rows = token_table.shape[0]
    full_width = token_table.shape[2]
    base_ids = neighbour_ids.reshape(-1).shape[0]
    slot_cap = max(2, 2 * base_ids // owners)
    flat_ids = neighbour_ids.reshape(-1)
    id_count = flat_ids.shape[0]
    slot, asked = slot_plan(flat_ids, owners, slot_cap, shard_rows)
    found = token_table[
        lax.all_to_all(
            asked.reshape(owners, slot_cap),
            ("seq", "heads"),
            split_axis=0,
            concat_axis=0,
            tiled=True,
        )
    ]
    returned = lax.all_to_all(found, ("seq", "heads"), split_axis=0, concat_axis=0, tiled=True)
    embedded = returned.reshape(owners * slot_cap, 2, full_width)[slot]
    encoded = encode_rows(embedded, id_count, full_width)
    encoded = lax.all_to_all(encoded, "heads", split_axis=3, concat_axis=0, tiled=True)
    previous = from_behind(encoded[-1:], "seq", 1)
    extended = jnp.concatenate([previous, encoded], axis=0)
    blocks = extended.shape[0]
    padded = jnp.pad(cca_queries, ((1, STRETCH - 1), (0, 0))).reshape(
        blocks, STRETCH, local_heads, HS
    )
    cross = attend(
        padded,
        extended[:, :, 0].reshape(blocks, NEIGH * NLEN, local_heads, HS),
        extended[:, :, 1].reshape(blocks, NEIGH * NLEN, local_heads, HS),
        jnp.ones((1, STRETCH, NEIGH * NLEN), bool),
    )
    cca_out = cross.reshape(blocks * STRETCH, width)[1 : 1 + tok_rows].astype(jnp.bfloat16)
    return (attention_out, cca_out)


def solution(mesh):
    in_specs = (
        P("seq", "heads"),
        P("seq", "heads"),
        P("seq", "heads"),
        P("seq", "heads"),
        P(("seq", "heads"), None, None),
        P(("seq", "heads"), None, None),
        P(),
    )
    out_specs = (P("seq", "heads"), P("seq", "heads"))
    return jax.shard_map(body, mesh=mesh, in_specs=in_specs, out_specs=out_specs, check_vma=False)
```

profile of v0, /device:TPU:16, one launch (start us, length us, event | category | flops | bytes accessed | tf_op | source)
XLA Modules:
  0.0 451.4 jit_solution(9298145688821688848)
XLA Ops:
  4.4 18.3 %all_to_all.35 = s32[128,1,4]{2,1,0:T(1,128)S(1)} all-to-all(s32[128,1,4]{2,1,0:T(1,128)S(1)} %bitcast.345), channel_id=1, replica_groups=mesh['seq'=32,'heads'=4] {'seq','heads'}, dimensions={0} | all-to-all | bytes 4096 | tf_op jit(solution)/shard_map/all_to_all | solution.py:117
  22.8 31.6 %gather_fusion = bf16[512,2,4096]{2,1,0:T(2,128)(2,1)} fusion(bf16[1000,2,4096]{2,1,0:T(2,128)(2,1)} %param.11, s32[1024]{0:T(1024)S(1)} %pad_clamp_fusion.1), kind=kCustom, calls=%fused_computation | custom fusion | bytes 16779264 | tf_op jit(solution)/shard_map/gather | solution.py:116
  54.4 6.9 %all-to-all-start.1 = ((bf16[128,4,2,4096]{3,2,1,0:T(2,128)(2,1)}), bf16[128,4,2,4096]{3,2,1,0:T(2,128)(2,1)}, u32[]{:S(2)}, u32[]{:S(2)}) async-start(bf16[128,4,2,4096]{3,2,1,0:T(2,128)(2,1)} %bitcast.308), calls=%async_computation.1 | async-start | bytes 16777216 | tf_op jit(solution)/shard_map/all_to_all | solution.py:125
  64.0 102.5 %collective-permute-done = bf16[2,256,1024]{1,2,0:T(8,128)(2,1)S(1)} collective-permute-done((bf16[2,256,1024]{1,2,0:T(8,128)(2,1)S(1)}, bf16[2,256,1024]{1,2,0:T(8,128)(2,1)S(1)}, u32[]{:S(2)}, u32[]{:S(2)}) %collective-permute-start) | collective-permute-done | bytes 1048608 | tf_op jit(solution)/shard_map/ppermute | solution.py:20
  169.5 16.3 %collective-permute-done.1 = bf16[2,256,1024]{1,2,0:T(8,128)(2,1)S(1)} collective-permute-done((bf16[2,256,1024]{1,2,0:T(8,128)(2,1)S(1)}, bf16[2,256,1024]{1,2,0:T(8,128)(2,1)S(1)}, u32[]{:S(2)}, u32[]{:S(2)}) %collective-permute-start.1) | collective-permute-done | bytes 1048608 | tf_op jit(solution)/shard_map/ppermute | solution.py:20
  188.7 16.3 %collective-permute-done.2 = bf16[2,256,1024]{1,2,0:T(8,128)(2,1)S(1)} collective-permute-done((bf16[2,256,1024]{1,2,0:T(8,128)(2,1)S(1)}, bf16[2,256,1024]{1,2,0:T(8,128)(2,1)S(1)}, u32[]{:S(2)}, u32[]{:S(2)}) %collective-permute-start.2) | collective-permute-done | bytes 1048608 | tf_op jit(solution)/shard_map/ppermute | solution.py:20
  207.8 16.3 %collective-permute-done.3 = bf16[2,256,1024]{1,2,0:T(8,128)(2,1)S(1)} collective-permute-done((bf16[2,256,1024]{1,2,0:T(8,128)(2,1)S(1)}, bf16[2,256,1024]{1,2,0:T(8,128)(2,1)S(1)}, u32[]{:S(2)}, u32[]{:S(2)}) %collective-permute-start.3) | collective-permute-done | bytes 1048608 | tf_op jit(solution)/shard_map/ppermute | solution.py:20
  227.0 16.3 %collective-permute-done.4 = bf16[2,256,1024]{1,2,0:T(8,128)(2,1)S(1)} collective-permute-done((bf16[2,256,1024]{1,2,0:T(8,128)(2,1)S(1)}, bf16[2,256,1024]{1,2,0:T(8,128)(2,1)S(1)}, u32[]{:S(2)}, u32[]{:S(2)}) %collective-permute-start.4) | collective-permute-done | bytes 1048608 | tf_op jit(solution)/shard_map/ppermute | solution.py:20
  246.5 15.2 %collective-permute-done.5 = bf16[2,256,1024]{1,2,0:T(8,128)(2,1)} collective-permute-done((bf16[2,256,1024]{1,2,0:T(8,128)(2,1)S(1)}, bf16[2,256,1024]{1,2,0:T(8,128)(2,1)}, u32[]{:S(2)}, u32[]{:S(2)}) %collective-permute-start.5) | collective-permute-done | bytes 1048608 | tf_op jit(solution)/shard_map/ppermute | solution.py:20
  270.0 10.2 %collective-permute-done.6 = bf16[2,256,1024]{1,2,0:T(8,128)(2,1)} collective-permute-done((bf16[2,256,1024]{1,2,0:T(8,128)(2,1)}, bf16[2,256,1024]{1,2,0:T(8,128)(2,1)}, u32[]{:S(2)}, u32[]{:S(2)}) %collective-permute-start.6) | collective-permute-done | bytes 1048608 | tf_op jit(solution)/shard_map/ppermute | solution.py:20
  286.0 17.5 %gather_fusion.1 = bf16[256,2,4096]{2,1,0:T(2,128)(2,1)} fusion(bf16[512,2,4096]{2,1,0:T(2,128)(2,1)} %bitcast.50, s32[1024]{0:T(1024)S(1)} %pad_clamp_fusion), kind=kCustom, calls=%fused_computation.1 | custom fusion | bytes 8389632 | tf_op jit(solution)/shard_map/gather | solution.py:126
  303.4 23.6 %slice_reduce_fusion.1 = (bf16[256,4096]{1,0:T(8,128)(2,1)}, bf16[256,4096]{1,0:T(8,128)(2,1)S(1)}, bf16[256,1,4096]{2,1,0:T(2,128)(2,1)}) fusion(bf16[256,2,4096]{2,1,0:T(2,128)(2,1)} %gather_fusion.1), kind=kLoop, calls=%fused_computation.156 | loop fusion | bytes 10485760 | tf_op jit(solution)/shard_map/slice | solution.py:59
  327.6 3.5 copy.194
  338.9 3.4 copy.199
  342.3 6.2 %stack_reshape.4 = bf16[256,1,4096]{2,1,0:T(2,128)(2,1)} reshape(bf16[2,128,32,128]{3,2,1,0:T(8,128)(2,1)S(1)} %copy.199) | data formatting | bytes 4194304 | tf_op jit(solution)/shard_map/stack;reshape | solution.py:63
  348.6 11.7 %maximum_bitcast_fusion = bf16[1,256,2,4096]{3,2,1,0:T(2,128)(2,1)} fusion(bf16[256,1,4096]{2,1,0:T(2,128)(2,1)} %stack_reshape.4, bf16[256,1,4096]{2,1,0:T(2,128)(2,1)} %get-tuple-element.24), kind=kLoop, calls=%fused_computation.10 | loop fusion | flops 8388608 | bytes 8388608 | tf_op jit(solution)/shard_map/reshape | solution.py:70
  360.3 14.9 %copy.201 = bf16[1,256,2,4096]{1,2,0,3:T(2,128)(2,1)} copy(bf16[1,256,2,4096]{3,2,1,0:T(2,128)(2,1)} %maximum_bitcast_fusion) | data formatting | bytes 8388608 | tf_op jit(solution)/shard_map/reshape | solution.py:70
  375.2 8.8 %all-to-all-start.2 = ((bf16[1,256,2,4096]{1,2,0,3:T(2,128)(2,1)}), bf16[1,256,2,4096]{1,2,0,3:T(2,128)(2,1)}, u32[]{:S(2)}, u32[]{:S(2)}) async-start(bf16[1,256,2,4096]{1,2,0,3:T(2,128)(2,1)} %copy.201), calls=%async_computation.2 | async-start | bytes 8388608 | tf_op jit(solution)/shard_map/all_to_all | solution.py:128
  389.6 6.1 %fusion.124 = (bf16[1,2048,1024]{1,2,0:T(8,128)(2,1)}, bf16[1,2048,1024]{1,2,0:T(8,128)(2,1)}) fusion(bf16[2,2048,1024]{1,2,0:T(8,128)(2,1)} %constant_dynamic-update-slice_fusion), kind=kLoop, calls=%fused_computation.157 | loop fusion | bytes 16777216 | tf_op jit(solution)/shard_map/slice | solution.py:95
  399.0 3.6 fusion.78
  406.0 3.6 fusion.75
  412.9 8.4 %all-to-all-done.2 = bf16[1,256,2,4096]{1,2,0,3:T(2,128)(2,1)} async-done(((bf16[1,256,2,4096]{1,2,0,3:T(2,128)(2,1)}), bf16[1,256,2,4096]{1,2,0,3:T(2,128)(2,1)}, u32[]{:S(2)}, u32[]{:S(2)}) %all-to-all-start.2) | async-done | bytes 4194336 | tf_op jit(solution)/shard_map/all_to_all | solution.py:128
  428.1 3.6 fusion.72
  435.1 4.2 fusion.69
  (96 shorter events, 81.2 us)
Async XLA Ops:
  54.4 6.9 %copy-start.11 = (bf16[256,1024]{1,0:T(8,128)(2,1)S(1)}, bf16[256,1024]{1,0:T(8,128)(2,1)}, u32[]{:S(2)}) copy-start(bf16[256,1024]{1,0:T(8,128)(2,1)} %param.9) | copy-start | bytes 1572868
  54.4 7.1 %copy-start.12 = (bf16[256,1024]{1,0:T(8,128)(2,1)S(1)}, bf16[256,1024]{1,0:T(8,128)(2,1)}, u32[]{:S(2)}) copy-start(bf16[256,1024]{1,0:T(8,128)(2,1)} %param.8) | copy-start | bytes 1572868
  54.4 231.6 %all-to-all-start.1 = ((bf16[128,4,2,4096]{3,2,1,0:T(2,128)(2,1)}), bf16[128,4,2,4096]{3,2,1,0:T(2,128)(2,1)}, u32[]{:S(2)}, u32[]{:S(2)}) async-start(bf16[128,4,2,4096]{3,2,1,0:T(2,128)(2,1)} %bitcast.308), calls=%async_computation.1 | async-start | bytes 16777216 | tf_op jit(solution)/shard_map/all_to_all | solution.py:125
  61.4 202.5 %copy-start.15 = (s32[32]{0:T(128)S(1)}, s32[32]{0:T(128)}, u32[]{:S(2)}) copy-start(s32[32]{0:T(128)} %param.13) | copy-start | bytes 388
  61.9 104.6 %collective-permute-start = (bf16[2,256,1024]{1,2,0:T(8,128)(2,1)S(1)}, bf16[2,256,1024]{1,2,0:T(8,128)(2,1)S(1)}, u32[]{:S(2)}, u32[]{:S(2)}) collective-permute-start(bf16[2,256,1024]{1,2,0:T(8,128)(2,1)S(1)} %pad_maximum_fusion.1), channel_id=1, source_target_pairs={{0,4},{4,8},{8,12},{12,16},{16,20},{20,24},{24,28},{28,32},{32,36}... | collective-permute-start | bytes 3145736 | tf_op jit(solution)/shard_map/ppermute | solution.py:20
  166.5 1.1 copy-start.3
  167.5 18.2 %collective-permute-start.1 = (bf16[2,256,1024]{1,2,0:T(8,128)(2,1)S(1)}, bf16[2,256,1024]{1,2,0:T(8,128)(2,1)S(1)}, u32[]{:S(2)}, u32[]{:S(2)}) collective-permute-start(bf16[2,256,1024]{1,2,0:T(8,128)(2,1)S(1)} %collective-permute-done), channel_id=1, source_target_pairs={{0,4},{4,8},{8,12},{12,16},{16,20},{20,24},{24,28},{28,32},{32,36}... | collective-permute-start | bytes 3145736 | tf_op jit(solution)/shard_map/ppermute | solution.py:20
  186.7 18.2 %collective-permute-start.2 = (bf16[2,256,1024]{1,2,0:T(8,128)(2,1)S(1)}, bf16[2,256,1024]{1,2,0:T(8,128)(2,1)S(1)}, u32[]{:S(2)}, u32[]{:S(2)}) collective-permute-start(bf16[2,256,1024]{1,2,0:T(8,128)(2,1)S(1)} %collective-permute-done.1), channel_id=1, source_target_pairs={{0,4},{4,8},{8,12},{12,16},{16,20},{20,24},{24,28},{28,32},{32,36}... | collective-permute-start | bytes 3145736 | tf_op jit(solution)/shard_map/ppermute | solution.py:20
  205.0 1.0 copy-start.7
  205.9 18.2 %collective-permute-start.3 = (bf16[2,256,1024]{1,2,0:T(8,128)(2,1)S(1)}, bf16[2,256,1024]{1,2,0:T(8,128)(2,1)S(1)}, u32[]{:S(2)}, u32[]{:S(2)}) collective-permute-start(bf16[2,256,1024]{1,2,0:T(8,128)(2,1)S(1)} %collective-permute-done.2), channel_id=1, source_target_pairs={{0,4},{4,8},{8,12},{12,16},{16,20},{20,24},{24,28},{28,32},{32,36}... | collective-permute-start | bytes 3145736 | tf_op jit(solution)/shard_map/ppermute | solution.py:20
  225.1 18.2 %collective-permute-start.4 = (bf16[2,256,1024]{1,2,0:T(8,128)(2,1)S(1)}, bf16[2,256,1024]{1,2,0:T(8,128)(2,1)S(1)}, u32[]{:S(2)}, u32[]{:S(2)}) collective-permute-start(bf16[2,256,1024]{1,2,0:T(8,128)(2,1)S(1)} %collective-permute-done.3), channel_id=1, source_target_pairs={{0,4},{4,8},{8,12},{12,16},{16,20},{20,24},{24,28},{28,32},{32,36}... | collective-permute-start | bytes 3145736 | tf_op jit(solution)/shard_map/ppermute | solution.py:20
  243.3 18.3 %collective-permute-start.5 = (bf16[2,256,1024]{1,2,0:T(8,128)(2,1)S(1)}, bf16[2,256,1024]{1,2,0:T(8,128)(2,1)}, u32[]{:S(2)}, u32[]{:S(2)}) collective-permute-start(bf16[2,256,1024]{1,2,0:T(8,128)(2,1)S(1)} %collective-permute-done.4), channel_id=1, source_target_pairs={{0,4},{4,8},{8,12},{12,16},{16,20},{20,24},{24,28},{28,32},{32,36}... | collective-permute-start | bytes 3145736 | tf_op jit(solution)/shard_map/ppermute | solution.py:20
  261.6 18.5 %collective-permute-start.6 = (bf16[2,256,1024]{1,2,0:T(8,128)(2,1)}, bf16[2,256,1024]{1,2,0:T(8,128)(2,1)}, u32[]{:S(2)}, u32[]{:S(2)}) collective-permute-start(bf16[2,256,1024]{1,2,0:T(8,128)(2,1)} %collective-permute-done.5), channel_id=1, source_target_pairs={{0,4},{4,8},{8,12},{12,16},{16,20},{20,24},{24,28},{28,32},{32,36}... | collective-permute-start | bytes 3145736 | tf_op jit(solution)/shard_map/ppermute | solution.py:20
  333.1 2.9 copy-start.2
  375.2 8.8 %copy-start.10 = (bf16[2,256,1024]{1,2,0:T(8,128)(2,1)S(1)}, bf16[2,256,1024]{1,2,0:T(8,128)(2,1)}, u32[]{:S(2)}) copy-start(bf16[2,256,1024]{1,2,0:T(8,128)(2,1)} %copy-done.9) | copy-start | bytes 3145732
  375.2 9.9 %copy-start.8 = (bf16[2,256,1024]{1,2,0:T(8,128)(2,1)S(1)}, bf16[2,256,1024]{1,2,0:T(8,128)(2,1)}, u32[]{:S(2)}) copy-start(bf16[2,256,1024]{1,2,0:T(8,128)(2,1)} %copy-done.7) | copy-start | bytes 3145732
  375.2 46.0 %all-to-all-start.2 = ((bf16[1,256,2,4096]{1,2,0,3:T(2,128)(2,1)}), bf16[1,256,2,4096]{1,2,0,3:T(2,128)(2,1)}, u32[]{:S(2)}, u32[]{:S(2)}) async-start(bf16[1,256,2,4096]{1,2,0,3:T(2,128)(2,1)} %copy.201), calls=%async_computation.2 | async-start | bytes 8388608 | tf_op jit(solution)/shard_map/all_to_all | solution.py:128
  384.0 2.3 copy-start.6
  384.0 3.4 copy-start.4
  389.6 6.1 %copy-start.13 = (bf16[256,1024]{0,1:T(8,128)(2,1)S(1)}, bf16[256,1024]{0,1:T(8,128)(2,1)}, u32[]{:S(2)}) copy-start(bf16[256,1024]{0,1:T(8,128)(2,1)} %copy.181) | copy-start | bytes 1572868
  389.6 6.1 %copy-start.14 = (pred[256,2048]{0,1:T(8,128)(4,1)S(1)}, pred[256,2048]{0,1:T(8,128)(4,1)}, u32[]{:S(2)}) copy-start(pred[256,2048]{0,1:T(8,128)(4,1)} %compare_and_fusion) | copy-start | bytes 1572868
  424.0 1.9 copy-start
  426.0 18.2 %collective-permute-start.7 = (bf16[1,256,2,1024]{1,3,0,2:T(8,128)(2,1)S(1)}, bf16[1,256,2,1024]{1,3,0,2:T(8,128)(2,1)S(1)}, u32[]{:S(2)}, u32[]{:S(2)}) collective-permute-start(bf16[1,256,2,1024]{1,3,0,2:T(8,128)(2,1)S(1)} %slice_bitcast_fusion), channel_id=1, source_target_pairs={{0,4},{4,8},{8,12},{12,16},{16,20},{20,24},{24,28},{28,32},{32,36}... | collective-permute-start | bytes 3145736 | tf_op jit(solution)/shard_map/ppermute | solution.py:20
  444.2 2.5 copy-start.1
  (2 other events, 1.9 us)
where the time goes:
time: 459 us; the launch traced here: 451 us
  waiting for transfers between devices  204 us (44%)
  local copies, waits for them, and re-layouts  137 us (30%)
  matrix products  35.1 us (8%)
  starting transfers between devices  31.6 us (7%)
  other arithmetic  23.5 us (5%)
  blocking collectives  18.3 us (4%)
    ppermute x8, waiting for transfers between devices, from_behind(): return lax.ppermute(block, axis, route)  196 us
    gather x1, local copies, waits for them, and re-layouts, body(): token_table[lax.all_to_all(asked.reshape(owners, slot_cap), ('seq', 'head...  31.6 us
    unnamed x48, local copies, waits for them, and re-layouts  24.5 us
    slice x1, local copies, waits for them, and re-layouts, encode_rows(): table_keys = embedded[:, 0].reshape(groups, NLEN, head_total, HS)  23.6 us
    dot_general x6, matrix products, attend(): jnp.einsum('bhqk,bkhd->bqhd', weights.astype(jnp.bfloat16), value_block,...  19.3 us
    all_to_all x1, blocking collectives, body(): lax.all_to_all(asked.reshape(owners, slot_cap), ('seq', 'heads'), split_a...  18.3 us
    gather x1, local copies, waits for them, and re-layouts, body(): embedded = returned.reshape(owners * slot_cap, 2, full_width)[slot]  17.5 us
    ppermute x8, starting transfers between devices, from_behind(): return lax.ppermute(block, axis, route)  15.9 us
  transfers between devices with their start and end apart: 10, of which 9 were waited for; matrix products, arithmetic and copies ran while one was open for 12% of the time, Pallas kernels for 0%

commit v1 on v0

v1 whole, which is shorter than its diff:
```python
import functools
import math

import jax
import jax.numpy as jnp
from jax import lax
from jax.experimental import pallas as pl
from jax.experimental.pallas import tpu as pltpu
from jax.sharding import PartitionSpec as P

MESH = pl.DeviceIdType.MESH
BF = jnp.bfloat16
F32 = jnp.float32
I32 = jnp.int32

HS = 128
STRETCH = 64
NLEN = 128
IDS = 256
CAP = 4
SEQ = 32
ZN = 4
DEV = SEQ * ZN
GROUP = 8
TOK = 256
HEADS_DEV = 8
SPAN = GROUP * TOK
HALO = 1792
WIN = HALO + TOK
WAVES = 8
PER_WAVE = SEQ // WAVES
NEG = -1e30
LOG2E = 1.4426950408889634
FACTOR = LOG2E / math.sqrt(HS)


def dot(a, b, contract=(1, 0)):
    return lax.dot_general(
        a, b, (((contract[0],), (contract[1],)), ((), ())), preferred_element_type=F32
    )


def iota(shape, dim):
    return lax.broadcasted_iota(I32, shape, dim)


def drain(ref, sem):
    pltpu.make_async_copy(ref, ref, sem).wait()


def kernel(
    q, k, v, cq, table, ids, lens, att, cca,
    tab, ids_all, plan_v, plan_s, send_buf, rows, zbuf, qh, kh, vh, oh, cqs, cqq, oc,
    tab_sem, id_send, id_recv, plan_sem, qkv_send, q_recv, k_recv, v_recv,
    halo_send, halo_recv, cq_send, cq_recv, row_send, row_recv,
    o_send, o_recv, oc_send, oc_recv,
):
    s = lax.axis_index("seq")
    z = lax.axis_index("heads")
    me = s * ZN + z
    y, x, c = s // 8, (s // 2) % 4, s % 2
    g = s % GROUP
    row = s // GROUP

    def place(y2, x2, c2):
        return (y2 * 4 + x2) * 2 + c2

    table_copy = pltpu.make_async_copy(table, tab, tab_sem)
    table_copy.start()

    barrier = pltpu.get_barrier_semaphore()

    def greet(i, carry):
        other = lax.rem(me + i, DEV)
        pl.semaphore_signal(
            barrier, inc=1, device_id=(other // ZN, lax.rem(other, ZN)), device_id_type=MESH
        )
        return carry

    lax.fori_loop(1, DEV, greet, 0)
    pl.semaphore_wait(barrier, DEV - 1)

    ids_all[me] = ids[0]
    first = []
    for n in range(1, 8):
        dc, dz = n // 4, n % 4
        s2, z2 = place(y, x, lax.rem(c + dc, 2)), lax.rem(z + dz, 4)
        copy = pltpu.make_async_remote_copy(
            ids_all.at[me], ids_all.at[me], id_send.at[n], id_recv.at[n],
            device_id=(s2, z2), device_id_type=MESH,
        )
        copy.start()
        first.append(copy)
    for copy in first:
        copy.wait()
    block = ids_all.at[pl.ds((y * 4 + x) * 8, 8)]
    second = []
    for n in range(1, 4):
        copy = pltpu.make_async_remote_copy(
            block, block, id_send.at[7 + n], id_recv.at[7 + n],
            device_id=(place(y, lax.rem(x + n, 4), c), z), device_id_type=MESH,
        )
        copy.start()
        second.append(copy)
    for copy in second:
        copy.wait()
    block = ids_all.at[pl.ds(y * 32, 32)]
    third = []
    for n in range(1, 4):
        copy = pltpu.make_async_remote_copy(
            block, block, id_send.at[10 + n], id_recv.at[10 + n],
            device_id=(place(lax.rem(y + n, 4), x, c), z), device_id_type=MESH,
        )
        copy.start()
        third.append(copy)

    for n in range(1, GROUP):
        to = lax.rem(g + n, GROUP)
        for src, dst, at, sem in (
            (q, qh, 0, q_recv), (k, kh, HALO, k_recv), (v, vh, HALO, v_recv),
        ):
            pltpu.make_async_remote_copy(
                src.at[:, pl.ds(to * HS, HS)], dst.at[pl.ds(at + g * TOK, TOK)],
                qkv_send, sem, device_id=(row * GROUP + to, z), device_id_type=MESH,
            ).start()
    for src, dst, at, sem in (
        (q, qh, 0, q_recv), (k, kh, HALO, k_recv), (v, vh, HALO, v_recv),
    ):
        pltpu.make_async_copy(
            src.at[:, pl.ds(g * HS, HS)], dst.at[pl.ds(at + g * TOK, TOK)], sem
        ).start()
    ahead = lax.rem(s + 1, SEQ)
    behind = lax.rem(s + SEQ - 1, SEQ)
    cq_copy = pltpu.make_async_remote_copy(
        cq.at[pl.ds(0, STRETCH)], cqs.at[pl.ds(TOK, STRETCH)], cq_send, cq_recv.at[0],
        device_id=(behind, z), device_id_type=MESH,
    )
    cq_copy.start()
    cq_own = pltpu.make_async_copy(cq, cqs.at[pl.ds(0, TOK)], cq_recv.at[1])
    cq_own.start()

    for copy in third:
        copy.wait()

    base = me * 1000
    row0 = ids_all[:, 0, :] - base
    row1 = ids_all[:, 1, :] - base
    mine0 = (row0 >= 0) & (row0 < 1000)
    mine1 = (row1 >= 0) & (row1 < 1000)
    flag0 = jnp.where(mine0, 1.0, 0.0).astype(BF)
    flag1 = jnp.where(mine1, 1.0, 0.0).astype(BF)
    tri = jnp.where(iota((HS, HS), 0) < iota((HS, HS), 1), 1.0, 0.0).astype(BF)
    full = jnp.ones((HS, HS), BF)
    rank0 = dot(flag0, tri)
    rank1 = dot(flag1, tri) + dot(flag0, full)
    plan = jnp.zeros((8, HS), I32)
    ones8 = jnp.ones((8, HS), BF)
    for n in range(CAP):
        pick = jnp.where(mine0 & (rank0 == float(n)), row0, 0) + jnp.where(
            mine1 & (rank1 == float(n)), row1, 0
        )
        high = dot(ones8, (pick >> 5).astype(F32).astype(BF), (1, 1))
        low = dot(ones8, (pick & 31).astype(F32).astype(BF), (1, 1))
        value = (high * 32.0 + low).astype(I32)
        plan = jnp.where(iota((8, HS), 0) == n, value, plan)
    plan_v[...] = plan
    plan_copy = pltpu.make_async_copy(plan_v, plan_s, plan_sem)
    plan_copy.start()
    plan_copy.wait()
    table_copy.wait()

    def column(t):
        dx = lax.rem(t, 4)
        dy = lax.rem(t // 4 + dx, 4)
        dc = t // 16
        return dx, dy, place(lax.rem(y + dy, 4), lax.rem(x + dx, 4), lax.rem(c + dc, 2))

    def fetch(to):
        for a in range(ZN):
            for n in range(CAP):
                found = tab[jnp.clip(plan_s[n, to * ZN + a], 0, 999)]
                send_buf[:, to, a, n * 16 : (n + 1) * 16, :] = found

    def post(to, z2, wave):
        pltpu.make_async_remote_copy(
            send_buf.at[z2, to], rows.at[:, me], row_send.at[wave], row_recv,
            device_id=(to, z2), device_id_type=MESH,
        ).start()

    def step(t, wave):
        dx, dy, to = column(t)
        fetch(to)
        for n in range(ZN):
            post(to, lax.rem(z + n + dx + dy, 4), wave)
        return wave

    fetch(s)
    pltpu.make_async_copy(send_buf.at[z, s], rows.at[:, me], row_recv).start()
    for n in range(1, ZN):
        post(s, lax.rem(z + n, 4), 0)
    lax.fori_loop(1, PER_WAVE, step, 0)

    def wave_out(wave):
        lax.fori_loop(wave * PER_WAVE, (wave + 1) * PER_WAVE, step, wave)

    wave_out(1)

    drain(qh, q_recv)
    drain(kh.at[pl.ds(HALO, SPAN)], k_recv)
    drain(vh.at[pl.ds(HALO, SPAN)], v_recv)
    next_row = lax.rem(row + 1, 4) * GROUP + g
    halos = []
    for n, ref in ((0, kh), (1, vh)):
        copy = pltpu.make_async_remote_copy(
            ref.at[pl.ds(HALO + TOK, HALO)], ref.at[pl.ds(0, HALO)],
            halo_send.at[n], halo_recv.at[n], device_id=(next_row, z), device_id_type=MESH,
        )
        copy.start()
        halos.append(copy)

    cq_copy.wait()
    cq_own.wait()
    up = jnp.where(iota((STRETCH, HS), 1) == iota((STRETCH, HS), 0) + 63, 1.0, 0.0).astype(BF)
    for a in range(4):
        moved = dot(up, cqs[a * STRETCH : a * STRETCH + 2 * STRETCH, :]).astype(BF)
        for h in range(HEADS_DEV):
            cqq[a, h] = moved[:, h * HS : (h + 1) * HS]

    for copy in halos:
        copy.wait()

    def self_block(i):
        first_query = row * SPAN + i * TOK
        query_pos = iota((1, TOK), 1) + first_query
        begin = jnp.zeros((1, TOK), I32)
        end = 0
        for d in range(32):
            end = end + lens[d]
            begin = jnp.where(query_pos >= end, end, begin)
        at = pl.multiple_of(i * TOK, TOK)
        key_pos = iota((WIN, TOK), 0) + (first_query - HALO)
        scores = dot(kh[pl.ds(at, WIN), :], qh[pl.ds(at, TOK), :], (1, 1))
        scores = jnp.where((key_pos >= begin) & (key_pos <= query_pos), scores, NEG)
        top = jnp.max(scores, axis=0, keepdims=True)
        weights = jnp.exp2((scores - top) * FACTOR)
        total = jnp.sum(weights, axis=0, keepdims=True)
        mixed = dot(vh[pl.ds(at, WIN), :], weights.astype(BF), (0, 0)) / total
        oh[pl.ds(at, TOK), :] = mixed.T.astype(BF)

    def self_out(i):
        at = pl.multiple_of(i * TOK, TOK)
        place_out = att.at[:, pl.ds(pl.multiple_of(g * HS, HS), HS)]

        @pl.when(i != g)
        def _():
            pltpu.make_async_remote_copy(
                oh.at[pl.ds(at, TOK)], place_out, o_send, o_recv,
                device_id=(row * GROUP + i, z), device_id_type=MESH,
            ).start()

        @pl.when(i == g)
        def _():
            pltpu.make_async_copy(oh.at[pl.ds(at, TOK)], place_out, o_recv).start()

    def wait_wave(wave):
        drain(send_buf.at[:, pl.ds(0, PER_WAVE)], row_send.at[wave])

    def turn(i, carry):
        self_block(i)
        self_out(i)

        @pl.when(i == 0)
        def _():
            drain(send_buf.at[0, pl.ds(0, 4 * PER_WAVE - 1)], row_send.at[0])

        @pl.when((i > 0) & (i < WAVES))
        def _():
            wait_wave(i)

        @pl.when(i + 2 < WAVES)
        def _():
            wave_out(i + 2)

        return carry

    lax.fori_loop(0, WAVES, turn, 0)

    drain(rows, row_recv)
    swap = jnp.where(
        (iota((256, 256), 0) // 16 == iota((256, 256), 1) % 16)
        & (iota((256, 256), 0) % 16 == iota((256, 256), 1) // 16),
        1.0, 0.0,
    ).astype(BF)

    def owner_of(value):
        return jnp.floor((value.astype(F32) + 0.5) * 0.001)

    def stretch(a):
        def turn_rows(n, carry):
            part = rows[a, pl.ds(n * 4, 4)].reshape(256, HS)
            turned = dot(swap, part).astype(BF)
            for h in range(HEADS_DEV):
                for kv in range(2):
                    piece = turned[(2 * h + kv) * 16 : (2 * h + kv + 1) * 16, :]
                    zbuf[h, pl.ds(n * 16, 16), kv * HS : (kv + 1) * HS] = piece
            return carry

        lax.fori_loop(0, 32, turn_rows, 0)
        wanted = ids_all[s * ZN + a]
        lane = [jnp.broadcast_to(owner_of(wanted[n : n + 1, :]), (HS, HS)) for n in range(2)]
        col = [jnp.transpose(w) for w in lane]
        before = iota((HS, HS), 1) < iota((HS, HS), 0)
        rank0 = jnp.sum(jnp.where((col[0] == lane[0]) & before, 1.0, 0.0), axis=1, keepdims=True)
        rank1 = jnp.sum(
            jnp.where((col[1] == lane[1]) & before, 1.0, 0.0)
            + jnp.where(col[1] == lane[0], 1.0, 0.0),
            axis=1, keepdims=True,
        )
        slot_no = iota((HS, DEV * CAP), 1).astype(F32)
        pick = jnp.concatenate(
            [
                jnp.where(slot_no == (owner[:, :1] * CAP + rank), 1.0, 0.0)
                for owner, rank in ((col[0], rank0), (col[1], rank1))
            ],
            axis=0,
        ).astype(BF)

        def heads(j, carry):
            for n in range(4):
                h = j * 4 + n
                both = dot(pick, zbuf[h]).astype(BF)
                keys, raw = both[:, :HS], both[:, HS:]
                encoded = []
                for m in range(2):
                    key, val = keys[m * NLEN : (m + 1) * NLEN], raw[m * NLEN : (m + 1) * NLEN]
                    scores = dot(key, key, (1, 1))
                    top = jnp.max(scores, axis=1, keepdims=True)
                    weights = jnp.exp2((scores - top) * FACTOR)
                    total = jnp.sum(weights, axis=1, keepdims=True)
                    mixed = dot(weights.astype(BF), val) / total
                    encoded.append((val.astype(F32) + mixed).astype(BF))
                vals = jnp.concatenate(encoded, axis=0)
                scores = dot(cqq[a, h], keys, (1, 1))
                top = jnp.max(scores, axis=1, keepdims=True)
                weights = jnp.exp2((scores - top) * FACTOR)
                total = jnp.sum(weights, axis=1, keepdims=True)
                oc[a + 1, h] = (dot(weights.astype(BF), vals) / total).astype(BF)
            return carry

        lax.fori_loop(0, 2, heads, 0)

    stretch(3)
    oc_copy = pltpu.make_async_remote_copy(
        oc.at[4], oc.at[0], oc_send, oc_recv, device_id=(ahead, z), device_id_type=MESH
    )
    oc_copy.start()

    def others(a, carry):
        stretch(a)
        return carry

    lax.fori_loop(0, 3, others, 0)
    oc_copy.wait()
    down = jnp.where(iota((STRETCH, HS), 1) == iota((STRETCH, HS), 0) + 1, 1.0, 0.0).astype(BF)
    for b in range(4):
        for h in range(HEADS_DEV):
            upper = oc[b, h]
            if b == 0:
                upper = jnp.where(s == 0, jnp.zeros_like(upper), upper)
            pair = jnp.concatenate([upper, oc[b + 1, h]], axis=0)
            cca[b * STRETCH : (b + 1) * STRETCH, h * HS : (h + 1) * HS] = dot(down, pair).astype(BF)

    drain(att, o_recv)
    for _ in range(GROUP - 1):
        drain(oh.at[pl.ds(0, TOK)], o_send)
    for _ in range(3):
        drain(qh.at[pl.ds(0, HALO)], qkv_send)


def body(queries, keys, values, cca_queries, token_table, neighbour_ids, doc_lengths):
    view = token_table.reshape(1000, 2, 32, HS).transpose(0, 2, 1, 3).reshape(1000, ZN, 16, HS)
    vmem = pl.BlockSpec(memory_space=pltpu.VMEM)
    hbm = pl.BlockSpec(memory_space=pl.ANY)
    smem = pl.BlockSpec(memory_space=pltpu.SMEM)
    dma = pltpu.SemaphoreType.DMA
    return pl.pallas_call(
        kernel,
        out_shape=[
            jax.ShapeDtypeStruct((TOK, HEADS_DEV * HS), BF),
            jax.ShapeDtypeStruct((TOK, HEADS_DEV * HS), BF),
        ],
        in_specs=[hbm, hbm, hbm, hbm, hbm, vmem, smem],
        out_specs=[hbm, vmem],
        scratch_shapes=[
            pltpu.VMEM((1000, ZN, 16, HS), BF),
            pltpu.VMEM((DEV, 2, HS), I32),
            pltpu.VMEM((8, HS), I32),
            pltpu.SMEM((8, HS), I32),
            pltpu.VMEM((ZN, SEQ, 4, 64, HS), BF),
            pltpu.VMEM((4, DEV, 64, HS), BF),
            pltpu.VMEM((HEADS_DEV, DEV * CAP, 2 * HS), BF),
            pltpu.VMEM((SPAN, HS), BF),
            pltpu.VMEM((HALO + SPAN, HS), BF),
            pltpu.VMEM((HALO + SPAN, HS), BF),
            pltpu.VMEM((SPAN, HS), BF),
            pltpu.VMEM((TOK + STRETCH, HEADS_DEV * HS), BF),
            pltpu.VMEM((4, HEADS_DEV, STRETCH, HS), BF),
            pltpu.VMEM((5, HEADS_DEV, STRETCH, HS), BF),
            dma, dma((14,)), dma((14,)), dma, dma, dma, dma, dma,
            dma((2,)), dma((2,)), dma, dma((2,)), dma((WAVES,)), dma,
            dma, dma, dma, dma,
        ],
        compiler_params=pltpu.CompilerParams(
            collective_id=0, has_side_effects=True, vmem_limit_bytes=60 * 1024 * 1024
        ),
        name="retrieval",
    )(queries, keys, values, cca_queries, view, neighbour_ids, doc_lengths)


def solution(mesh):
    in_specs = (
        P("seq", "heads"),
        P("seq", "heads"),
        P("seq", "heads"),
        P("seq", "heads"),
        P(("seq", "heads"), None, None),
        P(("seq", "heads"), None, None),
        P(),
    )
    out_specs = (P("seq", "heads"), P("seq", "heads"))

    def run(*args):
        return tuple(
            jax.shard_map(body, mesh=mesh, in_specs=in_specs, out_specs=out_specs, check_vma=False)(*args)
        )

    return run
```

time: 459 us -> 233 us (0.51)
  the two profiles are of different devices: /device:TPU:16 before, /device:TPU:28 now
where the time goes in v1:
time: 233 us
  Pallas kernels  229 us (98%)
  local copies, waits for them, and re-layouts  3.74 us (2%)
    pallas_call x1, Pallas kernels, body(): pl.pallas_call(kernel, out_shape=[jax.ShapeDtypeStruct((TOK, HEADS_DEV *...  229 us

profile of v1, /device:TPU:28, one launch (start us, length us, event | category | flops | bytes accessed | tf_op | source)
XLA Modules:
  0.0 233.1 jit_solution(10618841960936385386)
XLA Ops:
  0.6 228.7 %retrieval.1 = (bf16[256,1024]{1,0:T(8,128)(2,1)}, bf16[256,1024]{1,0:T(8,128)(2,1)}) custom-call(bf16[256,1024]{1,0:T(8,128)(2,1)} %q.1, bf16[256,1024]{1,0:T(8,128)(2,1)} %k.1, bf16[256,1024]{1,0:T(8,128)(2,1)} %v.1, bf16[256,1024]{1,0:T(8,128)(2,1)} %cq.1, bf16[1000,4,16,128]{3,2,1,0:T(8,128)(2,1)} %bitcast.5, s32[1,2,128]{2,1,0:T(2,128)} %ids.1, s32[32]{0:T(128)} %lens.1), custom_call_target="tpu_custom_call" | custom-call | tf_op jit(solution)/shard_map/retrieval/pallas_call | solution.py:386
  229.4 1.9 copy.12
  231.3 1.9 copy.13

commit v2 on v1

--- a/solution.py
+++ b/solution.py
@@ -27,8 +27,6 @@
 SPAN = GROUP * TOK
 HALO = 1792
 WIN = HALO + TOK
-WAVES = 8
-PER_WAVE = SEQ // WAVES
 NEG = -1e30
 LOG2E = 1.4426950408889634
 FACTOR = LOG2E / math.sqrt(HS)
@@ -48,9 +46,12 @@
     pltpu.make_async_copy(ref, ref, sem).wait()
 
 
+ORDERS = (("y", "z", "x"), ("z", "x", "y"), ("x", "y", "z"), ("x", "y", "z"))
+
+
 def kernel(
     q, k, v, cq, table, ids, lens, att, cca,
-    tab, ids_all, plan_v, plan_s, send_buf, rows, zbuf, qh, kh, vh, oh, cqs, cqq, oc,
+    tab, ids_all, plan_v, plan_s, out1, in1, in2, rows, picks, zbuf, qh, kh, vh, oh, cqs, cqq, oc,
     tab_sem, id_send, id_recv, plan_sem, qkv_send, q_recv, k_recv, v_recv,
     halo_send, halo_recv, cq_send, cq_recv, row_send, row_recv,
     o_send, o_recv, oc_send, oc_recv,
@@ -58,61 +59,54 @@
     s = lax.axis_index("seq")
     z = lax.axis_index("heads")
     me = s * ZN + z
-    y, x, c = s // 8, (s // 2) % 4, s % 2
-    g = s % GROUP
-    row = s // GROUP
-
-    def place(y2, x2, c2):
-        return (y2 * 4 + x2) * 2 + c2
+    y, x, c = s // 8, lax.rem(s // 2, 4), lax.rem(s, 2)
+    here = {"x": x, "y": y, "z": z}
+    g = lax.rem(s, GROUP)
+    row = y
+    ahead = lax.rem(s + 1, SEQ)
+    behind = lax.rem(s + SEQ - 1, SEQ)
+
+    def device(x2=x, y2=y, z2=z, c2=c):
+        return (y2 * 4 + x2) * 2 + c2, z2
+
+    def along(axis, n, dc=0):
+        to = lax.rem(here[axis] + n, 4)
+        return to, device(**{axis + "2": to, "c2": lax.rem(c + dc, 2)})
 
     table_copy = pltpu.make_async_copy(table, tab, tab_sem)
     table_copy.start()
 
     barrier = pltpu.get_barrier_semaphore()
-
-    def greet(i, carry):
-        other = lax.rem(me + i, DEV)
-        pl.semaphore_signal(
-            barrier, inc=1, device_id=(other // ZN, lax.rem(other, ZN)), device_id_type=MESH
-        )
-        return carry
-
-    lax.fori_loop(1, DEV, greet, 0)
-    pl.semaphore_wait(barrier, DEV - 1)
+    partners = [along("x", 0, 1)[1]]
+    for axis in ("x", "y", "z"):
+        for n in range(1, 4):
+            for dc in range(2):
+                partners.append(along(axis, n, dc)[1])
+    partners += [(ahead, z), (behind, z)]
+    for other in partners:
+        pl.semaphore_signal(barrier, inc=1, device_id=other, device_id_type=MESH)
+    pl.semaphore_wait(barrier, len(partners))
 
     ids_all[me] = ids[0]
-    first = []
-    for n in range(1, 8):
-        dc, dz = n // 4, n % 4
-        s2, z2 = place(y, x, lax.rem(c + dc, 2)), lax.rem(z + dz, 4)
+
+    def share(block, to, n):
         copy = pltpu.make_async_remote_copy(
-            ids_all.at[me], ids_all.at[me], id_send.at[n], id_recv.at[n],
-            device_id=(s2, z2), device_id_type=MESH,
+            block, block, id_send.at[n], id_recv.at[n], device_id=to, device_id_type=MESH
         )
         copy.start()
-        first.append(copy)
+        return copy
+
+    first = [
+        share(ids_all.at[me], along("z", n % 4, n // 4)[1], n) for n in range(1, 8)
+    ]
     for copy in first:
         copy.wait()
     block = ids_all.at[pl.ds((y * 4 + x) * 8, 8)]
-    second = []
-    for n in range(1, 4):
-        copy = pltpu.make_async_remote_copy(
-            block, block, id_send.at[7 + n], id_recv.at[7 + n],
-            device_id=(place(y, lax.rem(x + n, 4), c), z), device_id_type=MESH,
-        )
-        copy.start()
-        second.append(copy)
+    second = [share(block, along("x", n)[1], 7 + n) for n in range(1, 4)]
     for copy in second:
         copy.wait()
     block = ids_all.at[pl.ds(y * 32, 32)]
-    third = []
-    for n in range(1, 4):
-        copy = pltpu.make_async_remote_copy(
-            block, block, id_send.at[10 + n], id_recv.at[10 + n],
-            device_id=(place(lax.rem(y + n, 4), x, c), z), device_id_type=MESH,
-        )
-        copy.start()
-        third.append(copy)
+    third = [share(block, along("y", n)[1], 10 + n) for n in range(1, 4)]
 
     for n in range(1, GROUP):
         to = lax.rem(g + n, GROUP)
@@ -129,8 +123,6 @@
         pltpu.make_async_copy(
             src.at[:, pl.ds(g * HS, HS)], dst.at[pl.ds(at + g * TOK, TOK)], sem
         ).start()
-    ahead = lax.rem(s + 1, SEQ)
-    behind = lax.rem(s + SEQ - 1, SEQ)
     cq_copy = pltpu.make_async_remote_copy(
         cq.at[pl.ds(0, STRETCH)], cqs.at[pl.ds(TOK, STRETCH)], cq_send, cq_recv.at[0],
         device_id=(behind, z), device_id_type=MESH,
@@ -169,51 +161,83 @@
     plan_copy.wait()
     table_copy.wait()
 
-    def column(t):
-        dx = lax.rem(t, 4)
-        dy = lax.rem(t // 4 + dx, 4)
-        dc = t // 16
-        return dx, dy, place(lax.rem(y + dy, 4), lax.rem(x + dx, 4), lax.rem(c + dc, 2))
-
-    def fetch(to):
-        for a in range(ZN):
+    def fetch(a):
+        order = ORDERS[a]
+
+        def column(t, carry):
+            spot = {"y": t // 8, "x": lax.rem(t // 2, 4), "z": slice(None)}
+            c2 = lax.rem(t, 2)
             for n in range(CAP):
-                found = tab[jnp.clip(plan_s[n, to * ZN + a], 0, 999)]
-                send_buf[:, to, a, n * 16 : (n + 1) * 16, :] = found
-
-    def post(to, z2, wave):
-        pltpu.make_async_remote_copy(
-            send_buf.at[z2, to], rows.at[:, me], row_send.at[wave], row_recv,
-            device_id=(to, z2), device_id_type=MESH,
-        ).start()
-
-    def step(t, wave):
-        dx, dy, to = column(t)
-        fetch(to)
-        for n in range(ZN):
-            post(to, lax.rem(z + n + dx + dy, 4), wave)
-        return wave
-
-    fetch(s)
-    pltpu.make_async_copy(send_buf.at[z, s], rows.at[:, me], row_recv).start()
-    for n in range(1, ZN):
-        post(s, lax.rem(z + n, 4), 0)
-    lax.fori_loop(1, PER_WAVE, step, 0)
-
-    def wave_out(wave):
-        lax.fori_loop(wave * PER_WAVE, (wave + 1) * PER_WAVE, step, wave)
-
-    wave_out(1)
+                found = tab[jnp.clip(plan_s[n, t * ZN + a], 0, 999)]
+                at = (a, spot[order[0]], c2, spot[order[1]], spot[order[2]])
+                out1[at + (slice(n * 16, (n + 1) * 16), slice(None))] = found
+            return carry
+
+        lax.fori_loop(0, SEQ, column, 0)
+
+    def travel(a, phase):
+        axis = ORDERS[a][phase]
+        send, recv = row_send.at[a, phase], row_recv.at[a, phase]
+        if phase == 0:
+            hops = [(n, dc) for n in range(4) for dc in range(2)]
+        else:
+            hops = [(n, 0) for n in range(4)]
+        for n, dc in hops[1:] + hops[:1]:
+            to, dev = along(axis, n, dc)
+            if phase == 0:
+                src, dst = out1.at[a, to, lax.rem(c + dc, 2)], in1.at[a, here[axis] * 2 + c]
+            elif phase == 1:
+                src, dst = in1.at[a, :, to], in2.at[a, here[axis]]
+            else:
+                src, dst = in2.at[a, :, :, to], rows.at[a, here[axis]]
+            if (n, dc) == (0, 0):
+                pltpu.make_async_copy(src, dst, recv).start()
+            else:
+                pltpu.make_async_remote_copy(
+                    src, dst, send, recv, device_id=dev, device_id_type=MESH
+                ).start()
+
+    landed = (in1, in2, rows)
+
+    def arrive(a, phase):
+        drain(landed[phase].at[a], row_recv.at[a, phase])
+
+    for a in (3, 0, 1):
+        fetch(a)
+        travel(a, 0)
+    fetch(2)
+
+    def owner_of(value):
+        return jnp.floor((value.astype(F32) + 0.5) * 0.001).astype(I32)
+
+    before = iota((HS, HS), 1) < iota((HS, HS), 0)
+    slot_no = iota((HS, DEV * CAP), 1).astype(F32)
+    for a in range(4):
+        wanted = owner_of(ids_all[s * ZN + a])
+        lane = [jnp.broadcast_to(wanted[n : n + 1, :], (HS, HS)) for n in range(2)]
+        col = [jnp.transpose(w) for w in lane]
+        rank0 = jnp.sum(jnp.where((col[0] == lane[0]) & before, 1.0, 0.0), axis=1, keepdims=True)
+        rank1 = jnp.sum(
+            jnp.where((col[1] == lane[1]) & before, 1.0, 0.0)
+            + jnp.where(col[1] == lane[0], 1.0, 0.0),
+            axis=1, keepdims=True,
+        )
+        for n, rank in ((0, rank0), (1, rank1)):
+            owner = col[n][:, :1]
+            part = {"z": owner & 3, "x": (owner >> 3) & 3, "y": owner >> 5}
+            order = ORDERS[a]
+            where = part[order[2]] * 32 + part[order[1]] * 8 + part[order[0]] * 2 + ((owner >> 2) & 1)
+            slot = where.astype(F32) * CAP + rank
+            picks[a, n * HS : (n + 1) * HS, :] = jnp.where(slot_no == slot, 1.0, 0.0).astype(BF)
 
     drain(qh, q_recv)
     drain(kh.at[pl.ds(HALO, SPAN)], k_recv)
     drain(vh.at[pl.ds(HALO, SPAN)], v_recv)
-    next_row = lax.rem(row + 1, 4) * GROUP + g
     halos = []
     for n, ref in ((0, kh), (1, vh)):
         copy = pltpu.make_async_remote_copy(
             ref.at[pl.ds(HALO + TOK, HALO)], ref.at[pl.ds(0, HALO)],
-            halo_send.at[n], halo_recv.at[n], device_id=(next_row, z), device_id_type=MESH,
+            halo_send.at[n], halo_recv.at[n], device_id=along("y", 1)[1], device_id_type=MESH,
         )
         copy.start()
         halos.append(copy)
@@ -225,6 +249,12 @@
         moved = dot(up, cqs[a * STRETCH : a * STRETCH + 2 * STRETCH, :]).astype(BF)
         for h in range(HEADS_DEV):
             cqq[a, h] = moved[:, h * HS : (h + 1) * HS]
+
+    for a, b in ((3, 2), (0, None), (1, None)):
+        arrive(a, 0)
+        travel(a, 1)
+        if b is not None:
+            travel(b, 0)
 
     for copy in halos:
         copy.wait()
@@ -262,68 +292,50 @@
         def _():
             pltpu.make_async_copy(oh.at[pl.ds(at, TOK)], place_out, o_recv).start()
 
-    def wait_wave(wave):
-        drain(send_buf.at[:, pl.ds(0, PER_WAVE)], row_send.at[wave])
-
     def turn(i, carry):
         self_block(i)
         self_out(i)
-
-        @pl.when(i == 0)
-        def _():
-            drain(send_buf.at[0, pl.ds(0, 4 * PER_WAVE - 1)], row_send.at[0])
-
-        @pl.when((i > 0) & (i < WAVES))
-        def _():
-            wait_wave(i)
-
-        @pl.when(i + 2 < WAVES)
-        def _():
-            wave_out(i + 2)
-
         return carry
 
-    lax.fori_loop(0, WAVES, turn, 0)
-
-    drain(rows, row_recv)
+    lax.fori_loop(0, 3, turn, 0)
+    arrive(3, 1)
+    travel(3, 2)
+    arrive(2, 0)
+    travel(2, 1)
+    arrive(0, 1)
+    travel(0, 2)
+    arrive(1, 1)
+    travel(1, 2)
+    lax.fori_loop(3, GROUP, turn, 0)
+    arrive(2, 1)
+    travel(2, 2)
+
     swap = jnp.where(
         (iota((256, 256), 0) // 16 == iota((256, 256), 1) % 16)
         & (iota((256, 256), 0) % 16 == iota((256, 256), 1) // 16),
         1.0, 0.0,
     ).astype(BF)
 
-    def owner_of(value):
-        return jnp.floor((value.astype(F32) + 0.5) * 0.001)
-
     def stretch(a):
         def turn_rows(n, carry):
-            part = rows[a, pl.ds(n * 4, 4)].reshape(256, HS)
-            turned = dot(swap, part).astype(BF)
-            for h in range(HEADS_DEV):
-                for kv in range(2):
-                    piece = turned[(2 * h + kv) * 16 : (2 * h + kv + 1) * 16, :]
-                    zbuf[h, pl.ds(n * 16, 16), kv * HS : (kv + 1) * HS] = piece
+            for m in range(2):
+                spot = n * 4 + 2 * m
+                parts = [
+                    rows[a, n // 2, lax.rem(n, 2) * 2 + m, j * 4 : (j + 1) * 4].reshape(256, HS)
+                    for j in range(2)
+                ]
+                turned = dot(swap, jnp.concatenate(parts, axis=1)).astype(BF)
+                for j in range(2):
+                    for h in range(HEADS_DEV):
+                        for kv in range(2):
+                            piece = turned[
+                                (2 * h + kv) * 16 : (2 * h + kv + 1) * 16, j * HS : (j + 1) * HS
+                            ]
+                            zbuf[h, pl.ds((spot + j) * 16, 16), kv * HS : (kv + 1) * HS] = piece
             return carry
 
-        lax.fori_loop(0, 32, turn_rows, 0)
-        wanted = ids_all[s * ZN + a]
-        lane = [jnp.broadcast_to(owner_of(wanted[n : n + 1, :]), (HS, HS)) for n in range(2)]
-        col = [jnp.transpose(w) for w in lane]
-        before = iota((HS, HS), 1) < iota((HS, HS), 0)
-        rank0 = jnp.sum(jnp.where((col[0] == lane[0]) & before, 1.0, 0.0), axis=1, keepdims=True)
-        rank1 = jnp.sum(
-            jnp.where((col[1] == lane[1]) & before, 1.0, 0.0)
-            + jnp.where(col[1] == lane[0], 1.0, 0.0),
-            axis=1, keepdims=True,
-        )
-        slot_no = iota((HS, DEV * CAP), 1).astype(F32)
-        pick = jnp.concatenate(
-            [
-                jnp.where(slot_no == (owner[:, :1] * CAP + rank), 1.0, 0.0)
-                for owner, rank in ((col[0], rank0), (col[1], rank1))
-            ],
-            axis=0,
-        ).astype(BF)
+        lax.fori_loop(0, 8, turn_rows, 0)
+        pick = picks[a]
 
         def heads(j, carry):
             for n in range(4):
@@ -349,17 +361,15 @@
 
         lax.fori_loop(0, 2, heads, 0)
 
+    arrive(3, 2)
     stretch(3)
     oc_copy = pltpu.make_async_remote_copy(
         oc.at[4], oc.at[0], oc_send, oc_recv, device_id=(ahead, z), device_id_type=MESH
     )
     oc_copy.start()
-
-    def others(a, carry):
+    for a in (0, 1, 2):
+        arrive(a, 2)
         stretch(a)
-        return carry
-
-    lax.fori_loop(0, 3, others, 0)
     oc_copy.wait()
     down = jnp.where(iota((STRETCH, HS), 1) == iota((STRETCH, HS), 0) + 1, 1.0, 0.0).astype(BF)
     for b in range(4):
@@ -375,6 +385,10 @@
         drain(oh.at[pl.ds(0, TOK)], o_send)
     for _ in range(3):
         drain(qh.at[pl.ds(0, HALO)], qkv_send)
+    for a in range(4):
+        drain(in1.at[a, pl.ds(0, 7)], row_send.at[a, 0])
+        drain(in2.at[a, pl.ds(0, 3)], row_send.at[a, 1])
+        drain(rows.at[a, pl.ds(0, 3)], row_send.at[a, 2])
 
 
 def body(queries, keys, values, cca_queries, token_table, neighbour_ids, doc_lengths):
@@ -396,8 +410,11 @@
             pltpu.VMEM((DEV, 2, HS), I32),
             pltpu.VMEM((8, HS), I32),
             pltpu.SMEM((8, HS), I32),
-            pltpu.VMEM((ZN, SEQ, 4, 64, HS), BF),
-            pltpu.VMEM((4, DEV, 64, HS), BF),
+            pltpu.VMEM((4, 4, 2, 4, 4, 64, HS), BF),
+            pltpu.VMEM((4, 8, 4, 4, 64, HS), BF),
+            pltpu.VMEM((4, 4, 8, 4, 64, HS), BF),
+            pltpu.VMEM((4, 4, 4, 8, 64, HS), BF),
+            pltpu.VMEM((4, IDS, DEV * CAP), BF),
             pltpu.VMEM((HEADS_DEV, DEV * CAP, 2 * HS), BF),
             pltpu.VMEM((SPAN, HS), BF),
             pltpu.VMEM((HALO + SPAN, HS), BF),
@@ -407,7 +424,7 @@
             pltpu.VMEM((4, HEADS_DEV, STRETCH, HS), BF),
             pltpu.VMEM((5, HEADS_DEV, STRETCH, HS), BF),
             dma, dma((14,)), dma((14,)), dma, dma, dma, dma, dma,
-            dma((2,)), dma((2,)), dma, dma((2,)), dma((WAVES,)), dma,
+            dma((2,)), dma((2,)), dma, dma((2,)), dma((4, 3)), dma((4, 3)),
             dma, dma, dma, dma,
         ],
         compiler_params=pltpu.CompilerParams(

time: 233 us -> 165 us (0.71)
  the two profiles are of different devices: /device:TPU:28 before, /device:TPU:0 now
where the time goes in v2:
time: 165 us; the launch traced here: 162 us
  Pallas kernels  158 us (96%)
  local copies, waits for them, and re-layouts  3.74 us (2%)
    pallas_call x1, Pallas kernels, body(): pl.pallas_call(kernel, out_shape=[jax.ShapeDtypeStruct((TOK, HEADS_DEV *...  158 us
    unnamed x2, local copies, waits for them, and re-layouts  3.74 us

profile of v2, /device:TPU:0, one launch (start us, length us, event | category | flops | bytes accessed | tf_op | source)
XLA Modules:
  0.0 162.4 jit_solution(2720341982769214129)
XLA Ops:
  0.6 158.0 %retrieval.1 = (bf16[256,1024]{1,0:T(8,128)(2,1)}, bf16[256,1024]{1,0:T(8,128)(2,1)}) custom-call(bf16[256,1024]{1,0:T(8,128)(2,1)} %q.1, bf16[256,1024]{1,0:T(8,128)(2,1)} %k.1, bf16[256,1024]{1,0:T(8,128)(2,1)} %v.1, bf16[256,1024]{1,0:T(8,128)(2,1)} %cq.1, bf16[1000,4,16,128]{3,2,1,0:T(8,128)(2,1)} %bitcast.5, s32[1,2,128]{2,1,0:T(2,128)} %ids.1, s32[32]{0:T(128)} %lens.1), custom_call_target="tpu_custom_call" | custom-call | tf_op jit(solution)/shard_map/retrieval/pallas_call | solution.py:400
  158.7 1.9 %copy.12 = bf16[256,1024]{1,0:T(8,128)(2,1)} copy(bf16[256,1024]{1,0:T(8,128)(2,1)} %get-tuple-element.4) | data formatting | bytes 1048576
  160.6 1.9 %copy.13 = bf16[256,1024]{1,0:T(8,128)(2,1)} copy(bf16[256,1024]{1,0:T(8,128)(2,1)} %get-tuple-element.5) | data formatting | bytes 1048576

commit v3 on v2

--- a/solution.py
+++ b/solution.py
@@ -46,7 +46,12 @@
     pltpu.make_async_copy(ref, ref, sem).wait()
 
 
-ORDERS = (("y", "z", "x"), ("z", "x", "y"), ("x", "y", "z"), ("x", "y", "z"))
+ROUTES = (("x", "y", "z"), ("y", "z", "x"), ("z", "x", "y"))
+GROUPS = ((0, 2), (2, 1), (3, 1))
+
+
+def route(a, n):
+    return ROUTES[(a + n) % 3]
 
 
 def kernel(
@@ -73,6 +78,9 @@
         to = lax.rem(here[axis] + n, 4)
         return to, device(**{axis + "2": to, "c2": lax.rem(c + dc, 2)})
 
+    def across(dy, dx):
+        return device(x2=lax.rem(x + dx, 4), y2=lax.rem(y + dy, 4))
+
     table_copy = pltpu.make_async_copy(table, tab, tab_sem)
     table_copy.start()
 
@@ -82,6 +90,7 @@
         for n in range(1, 4):
             for dc in range(2):
                 partners.append(along(axis, n, dc)[1])
+    partners += [across(dy, dx) for dy in range(1, 4) for dx in range(1, 4)]
     partners += [(ahead, z), (behind, z)]
     for other in partners:
         pl.semaphore_signal(barrier, inc=1, device_id=other, device_id_type=MESH)
@@ -102,11 +111,7 @@
     for copy in first:
         copy.wait()
     block = ids_all.at[pl.ds((y * 4 + x) * 8, 8)]
-    second = [share(block, along("x", n)[1], 7 + n) for n in range(1, 4)]
-    for copy in second:
-        copy.wait()
-    block = ids_all.at[pl.ds(y * 32, 32)]
-    third = [share(block, along("y", n)[1], 10 + n) for n in range(1, 4)]
+    second = [share(block, across(n // 4, n % 4), 7 + n) for n in range(1, 16)]
 
     for n in range(1, GROUP):
         to = lax.rem(g + n, GROUP)
@@ -131,7 +136,7 @@
     cq_own = pltpu.make_async_copy(cq, cqs.at[pl.ds(0, TOK)], cq_recv.at[1])
     cq_own.start()
 
-    for copy in third:
+    for copy in second:
         copy.wait()
 
     base = me * 1000
@@ -162,45 +167,55 @@
     table_copy.wait()
 
     def fetch(a):
-        order = ORDERS[a]
-
         def column(t, carry):
             spot = {"y": t // 8, "x": lax.rem(t // 2, 4), "z": slice(None)}
             c2 = lax.rem(t, 2)
-            for n in range(CAP):
-                found = tab[jnp.clip(plan_s[n, t * ZN + a], 0, 999)]
+            for i, (low, count) in enumerate(GROUPS):
+                order = route(a, i)
                 at = (a, spot[order[0]], c2, spot[order[1]], spot[order[2]])
-                out1[at + (slice(n * 16, (n + 1) * 16), slice(None))] = found
+                for n in range(low, low + count):
+                    found = tab[jnp.clip(plan_s[n, t * ZN + a], 0, 999)]
+                    out1[at + (slice(n * 16, (n + 1) * 16), slice(None))] = found
             return carry
 
         lax.fori_loop(0, SEQ, column, 0)
 
+    def part_of(i):
+        low, count = GROUPS[i]
+        return pl.ds(low * 16, count * 16)
+
     def travel(a, phase):
-        axis = ORDERS[a][phase]
-        send, recv = row_send.at[a, phase], row_recv.at[a, phase]
-        if phase == 0:
-            hops = [(n, dc) for n in range(4) for dc in range(2)]
-        else:
-            hops = [(n, 0) for n in range(4)]
-        for n, dc in hops[1:] + hops[:1]:
-            to, dev = along(axis, n, dc)
+        everything = slice(None)
+        for i in range(3):
+            axis, part = route(a, i)[phase], part_of(i)
+            send, recv = row_send.at[a, phase, i], row_recv.at[a, phase, i]
             if phase == 0:
-                src, dst = out1.at[a, to, lax.rem(c + dc, 2)], in1.at[a, here[axis] * 2 + c]
-            elif phase == 1:
-                src, dst = in1.at[a, :, to], in2.at[a, here[axis]]
+                hops = [(n, dc) for n in range(4) for dc in range(2)]
             else:
-                src, dst = in2.at[a, :, :, to], rows.at[a, here[axis]]
-            if (n, dc) == (0, 0):
-                pltpu.make_async_copy(src, dst, recv).start()
-            else:
-                pltpu.make_async_remote_copy(
-                    src, dst, send, recv, device_id=dev, device_id_type=MESH
-                ).start()
+                hops = [(n, 0) for n in range(4)]
+            for n, dc in hops[1:] + hops[:1]:
+                to, dev = along(axis, n, dc)
+                if phase == 0:
+                    src = out1.at[a, to, lax.rem(c + dc, 2), :, :, part]
+                    dst = in1.at[a, here[axis] * 2 + c, :, :, part]
+                elif phase == 1:
+                    src = in1.at[a, :, to, :, part]
+                    dst = in2.at[a, here[axis], :, :, part]
+                else:
+                    src = in2.at[a, :, :, to, part]
+                    dst = rows.at[a, here[axis], :, :, part]
+                if (n, dc) == (0, 0):
+                    pltpu.make_async_copy(src, dst, recv).start()
+                else:
+                    pltpu.make_async_remote_copy(
+                        src, dst, send, recv, device_id=dev, device_id_type=MESH
+                    ).start()
 
     landed = (in1, in2, rows)
 
     def arrive(a, phase):
-        drain(landed[phase].at[a], row_recv.at[a, phase])
+        for i in range(3):
+            drain(landed[phase].at[a, :, :, :, part_of(i)], row_recv.at[a, phase, i])
 
     for a in (3, 0, 1):
         fetch(a)
@@ -225,9 +240,13 @@
         for n, rank in ((0, rank0), (1, rank1)):
             owner = col[n][:, :1]
             part = {"z": owner & 3, "x": (owner >> 3) & 3, "y": owner >> 5}
-            order = ORDERS[a]
-            where = part[order[2]] * 32 + part[order[1]] * 8 + part[order[0]] * 2 + ((owner >> 2) & 1)
-            slot = where.astype(F32) * CAP + rank
+            spots = []
+            for i in range(3):
+                order = route(a, i)
+                spot = part[order[2]] * 32 + part[order[1]] * 8 + part[order[0]] * 2
+                spots.append((spot + ((owner >> 2) & 1)).astype(F32))
+            spot = jnp.where(rank < 2.0, spots[0], jnp.where(rank < 3.0, spots[1], spots[2]))
+            slot = spot * CAP + rank
             picks[a, n * HS : (n + 1) * HS, :] = jnp.where(slot_no == slot, 1.0, 0.0).astype(BF)
 
     drain(qh, q_recv)
@@ -250,11 +269,13 @@
         for h in range(HEADS_DEV):
             cqq[a, h] = moved[:, h * HS : (h + 1) * HS]
 
-    for a, b in ((3, 2), (0, None), (1, None)):
-        arrive(a, 0)
-        travel(a, 1)
-        if b is not None:
-            travel(b, 0)
+    def onward(a, phase):
+        arrive(a, phase)
+        travel(a, phase + 1)
+
+    onward(3, 0)
+    travel(2, 0)
+    onward(0, 0)
 
     for copy in halos:
         copy.wait()
@@ -297,18 +318,13 @@
         self_out(i)
         return carry
 
-    lax.fori_loop(0, 3, turn, 0)
-    arrive(3, 1)
-    travel(3, 2)
-    arrive(2, 0)
-    travel(2, 1)
-    arrive(0, 1)
-    travel(0, 2)
-    arrive(1, 1)
-    travel(1, 2)
-    lax.fori_loop(3, GROUP, turn, 0)
-    arrive(2, 1)
-    travel(2, 2)
+    lax.fori_loop(0, 2, turn, 0)
+    onward(3, 1)
+    lax.fori_loop(2, 4, turn, 0)
+    onward(1, 0)
+    lax.fori_loop(4, 6, turn, 0)
+    onward(0, 1)
+    lax.fori_loop(6, 8, turn, 0)
 
     swap = jnp.where(
         (iota((256, 256), 0) // 16 == iota((256, 256), 1) % 16)
@@ -318,10 +334,10 @@
 
     def stretch(a):
         def turn_rows(n, carry):
-            for m in range(2):
-                spot = n * 4 + 2 * m
+            for m in range(8):
+                spot = n * 16 + 2 * m
                 parts = [
-                    rows[a, n // 2, lax.rem(n, 2) * 2 + m, j * 4 : (j + 1) * 4].reshape(256, HS)
+                    rows[a, n * 2 + m // 4, m % 4, j * 4 : (j + 1) * 4].reshape(256, HS)
                     for j in range(2)
                 ]
                 turned = dot(swap, jnp.concatenate(parts, axis=1)).astype(BF)
@@ -334,42 +350,47 @@
                             zbuf[h, pl.ds((spot + j) * 16, 16), kv * HS : (kv + 1) * HS] = piece
             return carry
 
-        lax.fori_loop(0, 8, turn_rows, 0)
+        lax.fori_loop(0, 2, turn_rows, 0)
         pick = picks[a]
 
-        def heads(j, carry):
-            for n in range(4):
-                h = j * 4 + n
-                both = dot(pick, zbuf[h]).astype(BF)
-                keys, raw = both[:, :HS], both[:, HS:]
-                encoded = []
-                for m in range(2):
-                    key, val = keys[m * NLEN : (m + 1) * NLEN], raw[m * NLEN : (m + 1) * NLEN]
-                    scores = dot(key, key, (1, 1))
-                    top = jnp.max(scores, axis=1, keepdims=True)
-                    weights = jnp.exp2((scores - top) * FACTOR)
-                    total = jnp.sum(weights, axis=1, keepdims=True)
-                    mixed = dot(weights.astype(BF), val) / total
-                    encoded.append((val.astype(F32) + mixed).astype(BF))
-                vals = jnp.concatenate(encoded, axis=0)
-                scores = dot(cqq[a, h], keys, (1, 1))
-                top = jnp.max(scores, axis=1, keepdims=True)
-                weights = jnp.exp2((scores - top) * FACTOR)
-                total = jnp.sum(weights, axis=1, keepdims=True)
-                oc[a + 1, h] = (dot(weights.astype(BF), vals) / total).astype(BF)
-            return carry
-
-        lax.fori_loop(0, 2, heads, 0)
+        def weigh(scores):
+            weights = jnp.exp2((scores - jnp.max(scores, axis=1, keepdims=True)) * FACTOR)
+            return weights, jnp.sum(weights, axis=1, keepdims=True)
+
+        both = [dot(pick, zbuf[h]).astype(BF) for h in range(HEADS_DEV)]
+        keys = [pair[:, :HS] for pair in both]
+        halves = [
+            [(pair[m * NLEN : (m + 1) * NLEN, :HS], pair[m * NLEN : (m + 1) * NLEN, HS:]) for m in range(2)]
+            for pair in both
+        ]
+        enc_scores = [[dot(key, key, (1, 1)) for key, _ in two] for two in halves]
+        cca_scores = [dot(cqq[a, h], keys[h], (1, 1)) for h in range(HEADS_DEV)]
+        enc = [[weigh(scores) for scores in two] for two in enc_scores]
+        cross = [weigh(scores) for scores in cca_scores]
+        for h in range(HEADS_DEV):
+            encoded = []
+            for (weights, total), (_, val) in zip(enc[h], halves[h]):
+                mixed = dot(weights.astype(BF), val) / total
+                encoded.append((val.astype(F32) + mixed).astype(BF))
+            weights, total = cross[h]
+            mixed = dot(weights.astype(BF), jnp.concatenate(encoded, axis=0)) / total
+            oc[a + 1, h] = mixed.astype(BF)
 
     arrive(3, 2)
+    onward(2, 0)
     stretch(3)
     oc_copy = pltpu.make_async_remote_copy(
         oc.at[4], oc.at[0], oc_send, oc_recv, device_id=(ahead, z), device_id_type=MESH
     )
     oc_copy.start()
-    for a in (0, 1, 2):
-        arrive(a, 2)
-        stretch(a)
+    onward(1, 1)
+    arrive(0, 2)
+    stretch(0)
+    onward(2, 1)
+    arrive(1, 2)
+    stretch(1)
+    arrive(2, 2)
+    stretch(2)
     oc_copy.wait()
     down = jnp.where(iota((STRETCH, HS), 1) == iota((STRETCH, HS), 0) + 1, 1.0, 0.0).astype(BF)
     for b in range(4):
@@ -386,9 +407,11 @@
     for _ in range(3):
         drain(qh.at[pl.ds(0, HALO)], qkv_send)
     for a in range(4):
-        drain(in1.at[a, pl.ds(0, 7)], row_send.at[a, 0])
-        drain(in2.at[a, pl.ds(0, 3)], row_send.at[a, 1])
-        drain(rows.at[a, pl.ds(0, 3)], row_send.at[a, 2])
+        for i in range(3):
+            part = part_of(i)
+            drain(in1.at[a, pl.ds(0, 7), :, :, part], row_send.at[a, 0, i])
+            drain(in2.at[a, pl.ds(0, 3), :, :, part], row_send.at[a, 1, i])
+            drain(rows.at[a, pl.ds(0, 3), :, :, part], row_send.at[a, 2, i])
 
 
 def body(queries, keys, values, cca_queries, token_table, neighbour_ids, doc_lengths):
@@ -423,12 +446,12 @@
             pltpu.VMEM((TOK + STRETCH, HEADS_DEV * HS), BF),
             pltpu.VMEM((4, HEADS_DEV, STRETCH, HS), BF),
             pltpu.VMEM((5, HEADS_DEV, STRETCH, HS), BF),
-            dma, dma((14,)), dma((14,)), dma, dma, dma, dma, dma,
-            dma((2,)), dma((2,)), dma, dma((2,)), dma((4, 3)), dma((4, 3)),
+            dma, dma((23,)), dma((23,)), dma, dma, dma, dma, dma,
+            dma((2,)), dma((2,)), dma, dma((2,)), dma((4, 3, 3)), dma((4, 3, 3)),
             dma, dma, dma, dma,
         ],
         compiler_params=pltpu.CompilerParams(
-            collective_id=0, has_side_effects=True, vmem_limit_bytes=60 * 1024 * 1024
+            collective_id=0, has_side_effects=True, vmem_limit_bytes=62 * 1024 * 1024
         ),
         name="retrieval",
     )(queries, keys, values, cca_queries, view, neighbour_ids, doc_lengths)

time: 165 us -> 143 us (0.87); the launches traced: 162 us -> 143 us
  Pallas kernels: 158 us -> 139 us
    pallas_call x1, Pallas kernels: 158 us -> 139 us  [body(): pl.pallas_call(kernel, out_shape=[jax.ShapeDtypeStruct((TOK, HEADS_DEV *...]
where the time goes in v3:
time: 143 us
  Pallas kernels  139 us (97%)
  local copies, waits for them, and re-layouts  3.74 us (3%)
    pallas_call x1, Pallas kernels, body(): pl.pallas_call(kernel, out_shape=[jax.ShapeDtypeStruct((TOK, HEADS_DEV *...  139 us
    unnamed x2, local copies, waits for them, and re-layouts  3.74 us

profile of v3, /device:TPU:0, one launch (start us, length us, event | category | flops | bytes accessed | tf_op | source)
XLA Modules:
  0.0 143.1 jit_solution(4726327788096820171)
XLA Ops:
  0.6 138.7 %retrieval.1 = (bf16[256,1024]{1,0:T(8,128)(2,1)}, bf16[256,1024]{1,0:T(8,128)(2,1)}) custom-call(bf16[256,1024]{1,0:T(8,128)(2,1)} %q.1, bf16[256,1024]{1,0:T(8,128)(2,1)} %k.1, bf16[256,1024]{1,0:T(8,128)(2,1)} %v.1, bf16[256,1024]{1,0:T(8,128)(2,1)} %cq.1, bf16[1000,4,16,128]{3,2,1,0:T(8,128)(2,1)} %bitcast.5, s32[1,2,128]{2,1,0:T(2,128)} %ids.1, s32[32]{0:T(128)} %lens.1), custom_call_target="tpu_custom_call" | custom-call | tf_op jit(solution)/shard_map/retrieval/pallas_call | solution.py:423
  139.3 1.9 %copy.12 = bf16[256,1024]{1,0:T(8,128)(2,1)} copy(bf16[256,1024]{1,0:T(8,128)(2,1)} %get-tuple-element.4) | data formatting | bytes 1048576
  141.2 1.9 %copy.13 = bf16[256,1024]{1,0:T(8,128)(2,1)} copy(bf16[256,1024]{1,0:T(8,128)(2,1)} %get-tuple-element.5) | data formatting | bytes 1048576

commit v4 on v3

--- a/solution.py
+++ b/solution.py
@@ -55,11 +55,11 @@
 
 
 def kernel(
-    q, k, v, cq, table, ids, lens, att, cca,
+    q, k, v, cq, table, ids, lens, att, done,
     tab, ids_all, plan_v, plan_s, out1, in1, in2, rows, picks, zbuf, qh, kh, vh, oh, cqs, cqq, oc,
     tab_sem, id_send, id_recv, plan_sem, qkv_send, q_recv, k_recv, v_recv,
     halo_send, halo_recv, cq_send, cq_recv, row_send, row_recv,
-    o_send, o_recv, oc_send, oc_recv,
+    o_send, o_recv, oc_send, oc_recv, done_sem,
 ):
     s = lax.axis_index("seq")
     z = lax.axis_index("heads")
@@ -376,9 +376,13 @@
             mixed = dot(weights.astype(BF), jnp.concatenate(encoded, axis=0)) / total
             oc[a + 1, h] = mixed.astype(BF)
 
+    def keep(n):
+        pltpu.make_async_copy(oc.at[n], done.at[n], done_sem).start()
+
     arrive(3, 2)
     onward(2, 0)
     stretch(3)
+    keep(4)
     oc_copy = pltpu.make_async_remote_copy(
         oc.at[4], oc.at[0], oc_send, oc_recv, device_id=(ahead, z), device_id_type=MESH
     )
@@ -386,20 +390,17 @@
     onward(1, 1)
     arrive(0, 2)
     stretch(0)
+    keep(1)
     onward(2, 1)
     arrive(1, 2)
     stretch(1)
+    keep(2)
     arrive(2, 2)
     stretch(2)
+    keep(3)
     oc_copy.wait()
-    down = jnp.where(iota((STRETCH, HS), 1) == iota((STRETCH, HS), 0) + 1, 1.0, 0.0).astype(BF)
-    for b in range(4):
-        for h in range(HEADS_DEV):
-            upper = oc[b, h]
-            if b == 0:
-                upper = jnp.where(s == 0, jnp.zeros_like(upper), upper)
-            pair = jnp.concatenate([upper, oc[b + 1, h]], axis=0)
-            cca[b * STRETCH : (b + 1) * STRETCH, h * HS : (h + 1) * HS] = dot(down, pair).astype(BF)
+    keep(0)
+    drain(done, done_sem)
 
     drain(att, o_recv)
     for _ in range(GROUP - 1):
@@ -414,20 +415,33 @@
             drain(rows.at[a, pl.ds(0, 3), :, :, part], row_send.at[a, 2, i])
 
 
+def finish(att_in, done, att, cca):
+    att[...] = att_in[...]
+    s = lax.axis_index("seq")
+    down = jnp.where(iota((STRETCH, HS), 1) == iota((STRETCH, HS), 0) + 1, 1.0, 0.0).astype(BF)
+    for b in range(4):
+        for h in range(HEADS_DEV):
+            upper = done[b, h]
+            if b == 0:
+                upper = jnp.where(s == 0, jnp.zeros_like(upper), upper)
+            pair = jnp.concatenate([upper, done[b + 1, h]], axis=0)
+            cca[b * STRETCH : (b + 1) * STRETCH, h * HS : (h + 1) * HS] = dot(down, pair).astype(BF)
+
+
 def body(queries, keys, values, cca_queries, token_table, neighbour_ids, doc_lengths):
     view = token_table.reshape(1000, 2, 32, HS).transpose(0, 2, 1, 3).reshape(1000, ZN, 16, HS)
     vmem = pl.BlockSpec(memory_space=pltpu.VMEM)
     hbm = pl.BlockSpec(memory_space=pl.ANY)
     smem = pl.BlockSpec(memory_space=pltpu.SMEM)
     dma = pltpu.SemaphoreType.DMA
-    return pl.pallas_call(
+    att, done = pl.pallas_call(
         kernel,
         out_shape=[
             jax.ShapeDtypeStruct((TOK, HEADS_DEV * HS), BF),
-            jax.ShapeDtypeStruct((TOK, HEADS_DEV * HS), BF),
+            jax.ShapeDtypeStruct((5, HEADS_DEV, STRETCH, HS), BF),
         ],
         in_specs=[hbm, hbm, hbm, hbm, hbm, vmem, smem],
-        out_specs=[hbm, vmem],
+        out_specs=[hbm, hbm],
         scratch_shapes=[
             pltpu.VMEM((1000, ZN, 16, HS), BF),
             pltpu.VMEM((DEV, 2, HS), I32),
@@ -448,13 +462,21 @@
             pltpu.VMEM((5, HEADS_DEV, STRETCH, HS), BF),
             dma, dma((23,)), dma((23,)), dma, dma, dma, dma, dma,
             dma((2,)), dma((2,)), dma, dma((2,)), dma((4, 3, 3)), dma((4, 3, 3)),
-            dma, dma, dma, dma,
+            dma, dma, dma, dma, dma,
         ],
         compiler_params=pltpu.CompilerParams(
             collective_id=0, has_side_effects=True, vmem_limit_bytes=62 * 1024 * 1024
         ),
         name="retrieval",
     )(queries, keys, values, cca_queries, view, neighbour_ids, doc_lengths)
+    out = jax.ShapeDtypeStruct((TOK, HEADS_DEV * HS), BF)
+    return pl.pallas_call(
+        finish,
+        out_shape=[out, out],
+        in_specs=[vmem, vmem],
+        out_specs=[vmem, vmem],
+        name="finish",
+    )(att, done)
 
 
 def solution(mesh):

time: 143 us -> 142 us (level)
  local copies, waits for them, and re-layouts: 3.74 us -> 0 us
  Pallas kernels: 139 us -> 141 us
    unnamed x2 -> x0, local copies, waits for them, and re-layouts: 3.74 us -> none
    pallas_call x0 -> x1, Pallas kernels: none -> 2.59 us  [body(): pl.pallas_call(finish, out_shape=[out, out], in_specs=[vmem, vmem], out_s...]
where the time goes in v4:
time: 142 us; the launch traced here: 141 us
  Pallas kernels  141 us (99%)
    pallas_call x1, Pallas kernels, body(): pl.pallas_call(kernel, out_shape=[jax.ShapeDtypeStruct((TOK, HEADS_DEV *...  138 us

profile of v4, /device:TPU:0, one launch (start us, length us, event | category | flops | bytes accessed | tf_op | source)
XLA Modules:
  0.0 141.4 jit_solution(3767616187971210140)
XLA Ops:
  0.6 138.2 %retrieval.1 = (bf16[256,1024]{1,0:T(8,128)(2,1)}, bf16[5,8,64,128]{3,2,1,0:T(8,128)(2,1)}) custom-call(bf16[256,1024]{1,0:T(8,128)(2,1)} %q.1, bf16[256,1024]{1,0:T(8,128)(2,1)} %k.1, bf16[256,1024]{1,0:T(8,128)(2,1)} %v.1, bf16[256,1024]{1,0:T(8,128)(2,1)} %cq.1, bf16[1000,4,16,128]{3,2,1,0:T(8,128)(2,1)} %bitcast.5, s32[1,2,128]{2,1,0:T(2,128)} %ids.1, ...), custom_call_target="tpu_custom_call" | custom-call | tf_op jit(solution)/shard_map/retrieval/pallas_call | solution.py:437
  138.8 2.6 %finish.1 = (bf16[256,1024]{1,0:T(8,128)(2,1)}, bf16[256,1024]{1,0:T(8,128)(2,1)}) custom-call(bf16[256,1024]{1,0:T(8,128)(2,1)} %get-tuple-element.4.att_in, bf16[5,8,64,128]{3,2,1,0:T(8,128)(2,1)} %get-tuple-element.5.done), custom_call_target="tpu_custom_call" | custom-call | tf_op jit(solution)/shard_map/finish/pallas_call | solution.py:473
